TPU v7x, 128 devices: a whole 4x4x4 slice. The times are simulated.
128 devices in a mesh: dp: 4 (over y), mp: 32 (over x, z, core).
Axes of the slice: x: 4, y: 4, z: 4, core: 2. Of those that a mesh axis runs over, the one named last changes fastest.
Arguments:
- residual_in: bfloat16 [512, 3584], P('dp', 'mp'), may hold values from -6 to 6
- pre_gain: float32 [3584], replicated, may hold values from 0.5 to 1.5
- post_gain: float32 [3584], replicated, may hold values from 0.5 to 1.5
- w_gate: bfloat16 [3584, 14336], P(None, 'mp'), may hold values from -0.09375 to 0.09375
- w_up: bfloat16 [3584, 14336], P(None, 'mp'), may hold values from -0.09375 to 0.09375
- w_down: bfloat16 [14336, 3584], P('mp'), may hold values from -0.046875 to 0.046875
- w_enc: bfloat16 [3584, 65536], P(None, ('dp', 'mp')), may hold values from -0.09375 to 0.09375
- b_enc: float32 [65536], P(('dp', 'mp')), may hold values from -2.5 to 2.5
- threshold: float32 [65536], P(('dp', 'mp')), may hold values from 0.1 to 1
- w_dec: bfloat16 [65536, 3584], P(('dp', 'mp')), may hold values from -0.0234375 to 0.0234375
- b_dec: float32 [3584], replicated, may hold values from -1.5 to 1.5
Outputs:
- loss_value: float32 [], replicated
- d_w_enc: bfloat16 [3584, 65536], P(None, ('dp', 'mp'))
- d_w_dec: bfloat16 [65536, 3584], P(('dp', 'mp'))
- d_b_enc: float32 [65536], P(('dp', 'mp'))
- d_threshold: float32 [65536], P(('dp', 'mp'))
- d_b_dec: float32 [3584], replicated
All inputs are finite; a program needn't handle non-finite values.
Results may differ from a plain program's by a relative error of at most 0.014.
The roundings to bfloat16 on the way count: a program that leaves them out, or rounds other values in their place, can miss the bound.
Values may be sent and summed in bfloat16 or wider, within the bound.
A program may use at most 128 MiB of HBM per device.

v0:
```python
import jax
import jax.numpy as jnp
from jax import lax
from jax.sharding import PartitionSpec as P

norm_eps = 1e-06
gate_band = 0.1
sparsity_coef = 0.05


def contract_first(left, right):
    return lax.dot_general(
        left, right, (((0,), (0,)), ((), ())), preferred_element_type=jnp.float32
    )


def local(
    residual_in, pre_gain, post_gain, w_gate, w_up, w_down, w_enc, b_enc, threshold, w_dec, b_dec
):
    full_rows = lax.all_gather(residual_in, "mp", axis=1, tiled=True)
    resid_wide = full_rows.astype(jnp.float32)
    normed = (
        resid_wide
        * lax.rsqrt(jnp.mean(resid_wide * resid_wide, axis=1, keepdims=True) + norm_eps)
        * pre_gain[None, :]
    ).astype(jnp.bfloat16)
    gate_out = jnp.dot(normed, w_gate, preferred_element_type=jnp.float32)
    up_out = jnp.dot(normed, w_up, preferred_element_type=jnp.float32)
    hidden = (jax.nn.gelu(gate_out, approximate=True) * up_out).astype(jnp.bfloat16)
    col_width = residual_in.shape[1]
    model_width = full_rows.shape[1]
    out_share = lax.psum_scatter(
        lax.dot_general(
            w_down, hidden, (((0,), (1,)), ((), ())), preferred_element_type=jnp.float32
        ),
        "mp",
        scatter_dimension=0,
        tiled=True,
    )
    total_sq = lax.psum(jnp.sum(out_share * out_share, axis=0), "mp")
    row_scale = lax.rsqrt(total_sq / model_width + norm_eps)
    my_cols = lax.axis_index("mp") * col_width
    gain_share = lax.dynamic_slice_in_dim(post_gain, my_cols, col_width, 0)
    mixed = residual_in.T.astype(jnp.float32) + out_share * row_scale[None, :] * gain_share[:, None]
    column_rows = lax.all_gather(mixed.astype(jnp.bfloat16), "mp", axis=0, tiled=True)
    h_cols = lax.all_gather(column_rows, "dp", axis=1, tiled=True)
    pre_act = contract_first(h_cols, w_enc) + b_enc[None, :]
    soft = jax.nn.sigmoid((pre_act - threshold[None, :]) / gate_band)
    feat_bf = (pre_act * soft).astype(jnp.bfloat16)
    gate_part = jnp.sum(soft)
    recon_part = lax.dot_general(
        w_dec, feat_bf, (((0,), (1,)), ((), ())), preferred_element_type=jnp.float32
    )
    recon_all, gate_total = lax.psum((recon_part, gate_part), ("dp", "mp"))
    error_t = recon_all + b_dec[:, None] - h_cols.astype(jnp.float32)
    grad_bdec = jnp.sum(error_t, axis=1)
    square_total = jnp.sum(error_t * error_t)
    err_bf = error_t.astype(jnp.bfloat16)
    loss_value = (0.5 * square_total + sparsity_coef * gate_total) / (
        h_cols.shape[0] * h_cols.shape[1]
    )
    grad_wdec = lax.dot_general(
        feat_bf, err_bf, (((0,), (1,)), ((), ())), preferred_element_type=jnp.float32
    ).astype(jnp.bfloat16)
    grad_feat = lax.dot_general(
        err_bf, w_dec, (((0,), (1,)), ((), ())), preferred_element_type=jnp.float32
    )
    slope = soft * (1.0 - soft) / gate_band
    side_term = (grad_feat * pre_act + sparsity_coef) * slope
    grad_pre = grad_feat * soft + side_term
    grad_thresh = -jnp.sum(side_term, axis=0)
    grad_benc = jnp.sum(grad_pre, axis=0)
    grad_wenc = jnp.dot(
        h_cols, grad_pre.astype(jnp.bfloat16), preferred_element_type=jnp.float32
    ).astype(jnp.bfloat16)
    return (loss_value, grad_wenc, grad_wdec, grad_benc, grad_thresh, grad_bdec)


def solution(mesh):
    placed = (
        P("dp", "mp"),
        P(),
        P(),
        P(None, "mp"),
        P(None, "mp"),
        P("mp", None),
        P(None, ("dp", "mp")),
        P(("dp", "mp")),
        P(("dp", "mp")),
        P(("dp", "mp"), None),
        P(),
    )
    return jax.shard_map(
        local,
        mesh=mesh,
        in_specs=placed,
        out_specs=(
            P(),
            P(None, ("dp", "mp")),
            P(("dp", "mp"), None),
            P(("dp", "mp")),
            P(("dp", "mp")),
            P(),
        ),
        check_vma=False,
    )
```

profile of v0, /device:TPU:1, one launch (start us, length us, event | category | flops | bytes accessed | tf_op | source)
XLA Modules:
  0.0 526.1 jit_solution(124205612583446622)
XLA Ops:
  7.2 0.0 copy-start
  7.2 0.0 reduce-scatter.4.cloned.1.call-start
  7.2 27.9 %all_gather.9 = bf16[128,3584]{0,1:T(8,128)(2,1)S(1)} all-gather(bf16[128,112]{0,1:T(8,128)(2,1)} %param.11), channel_id=1, replica_groups=mesh['dp'=4,'mp'=32] {'mp'}, dimensions={1}, use_global_device_ids=true | all-gather | bytes 946176 | tf_op jit(solution)/shard_map/all_gather | solution.py:20
  35.1 0.0 copy-start.1
  35.1 0.0 copy-start.3
  35.1 0.5 fusion.2
  35.6 0.4 copy-done.1
  36.0 3.1 fusion.20
  39.1 0.0 copy-done
  39.1 0.0 copy-done.3
  39.1 6.0 %convolution_bitcast_fusion.1 = f32[3584,128]{0,1:T(8,128)} fusion(bf16[448,3584]{1,0:T(8,128)(2,1)S(1)} %copy-done, f32[128,448]{0,1:T(8,128)S(1)} %fusion.20, bf16[3584,448]{0,1:T(8,128)(2,1)} %param.15, bf16[128,3584]{0,1:T(8,128)(2,1)} %copy-done.1, f32[3584]{0:T(1024)S(1)} %copy-done.3, f32[128]{0:T(128)S(1)} %add_rsqrt_fusion.1), kind=kOutput, calls=%fused_computation.5 | convolution fusion | flops 824033280 | bytes 9419264 | tf_op jit(solution)/shard_map/dot_general | solution.py:33
  45.1 0.0 copy-start.2
  45.1 2.7 copy.23
  47.8 0.0 copy-start.7
  47.8 0.0 reduce-scatter.4.cloned.1.call-update
  47.8 0.0 all-gather.2.cloned.1.call-start
  47.9 0.8 dynamic_slice.3
  48.6 75.3 %reduce-scatter.4.cloned.1.call-done = f32[112,128]{1,0:T(8,128)} async-done(((f32[3584,128]{1,0:T(8,128)}), f32[112,128]{1,0:T(8,128)}) %reduce-scatter.4.cloned.1.call-update) | async-done | bytes 57360 | tf_op jit(solution)/shard_map/reduce_scatter | solution.py:32
  123.9 0.9 copy.24
  124.8 0.1 multiply_reduce_fusion.1
  124.9 64.3 %psum.21 = f32[128]{0:T(128)S(1)} all-reduce(f32[128]{0:T(128)S(1)} %multiply_reduce_fusion.1), channel_id=1, replica_groups=mesh['dp'=4,'mp'=32] {'mp'}, use_global_device_ids=true, to_apply=%region_3.0 | all-reduce | flops 128 | bytes 1024 | tf_op jit(solution)/shard_map/psum | solution.py:40
  189.3 0.0 copy-done.2
  189.3 0.9 fusion.23
  190.2 25.7 %all_gather.10 = bf16[3584,128]{1,0:T(8,128)(2,1)} all-gather(bf16[112,128]{1,0:T(8,128)(2,1)S(1)} %fusion.23), channel_id=1, replica_groups=mesh['dp'=4,'mp'=32] {'mp'}, dimensions={0}, use_global_device_ids=true | all-gather | bytes 946176 | tf_op jit(solution)/shard_map/all_gather | solution.py:45
  215.9 2.2 copy.22
  218.1 0.0 all-gather.2.cloned.1.call-update
  218.1 0.0 copy-start.8
  218.1 0.2 all-reduce.2.cloned.1.call-start
  218.3 42.6 %all-gather.2.cloned.1.call-done = bf16[3584,512]{0,1:T(8,128)(2,1)} async-done(((bf16[3584,128]{0,1:T(8,128)(2,1)}), bf16[3584,512]{0,1:T(8,128)(2,1)}) %all-gather.2.cloned.1.call-update) | async-done | bytes 3670032 | tf_op jit(solution)/shard_map/all_gather | solution.py:46
  260.9 0.0 copy-done.7
  260.9 0.0 copy-start.5
  260.9 5.3 %convolution_add_fusion = f32[512,512]{1,0:T(8,128)S(1)} fusion(bf16[3584,512]{0,1:T(8,128)(2,1)} %all-gather.2.cloned.1.call-done, bf16[3584,512]{1,0:T(8,128)(2,1)} %param.17, f32[512]{0:T(512)S(1)} %copy-done.7), kind=kOutput, calls=%fused_computation.14 | convolution fusion | flops 1879310336 | bytes 8390656 | tf_op jit(solution)/shard_map/dot_general | solution.py:12
  266.3 0.0 copy-start.9
  266.3 1.0 copy-done.9
  267.2 0.0 copy-done.8
  267.2 0.0 copy-done.5
  267.2 5.1 convolution_bitcast_fusion
  272.4 0.0 copy-start.4
  272.4 0.0 all-reduce.2.cloned.1.call-update
  272.4 160.2 %all-reduce.2.cloned.1.call-done = f32[3584,512]{0,1:T(8,128)} async-done(((f32[3584,512]{0,1:T(8,128)}), f32[3584,512]{0,1:T(8,128)}) %all-reduce.2.cloned.1.call-update) | async-done | bytes 7340048 | tf_op jit(solution)/shard_map/psum | solution.py:54
  432.6 0.0 copy-done.4
  432.6 0.0 copy-start.6
  432.6 0.0 copy-start.10
  432.6 5.9 %fusion = (f32[3584]{0:T(1024)}, f32[]{:T(128)}, bf16[3584,512]{0,1:T(8,128)(2,1)S(1)}) fusion(bf16[3584,512]{0,1:T(8,128)(2,1)} %all-gather.2.cloned.1.call-done, f32[3584,512]{0,1:T(8,128)} %all-reduce.2.cloned.1.call-done, f32[3584]{0:T(1024)S(1)} %copy-done.4), kind=kLoop, calls=%fused_computation.8 | loop fusion | flops 12841471 | bytes 14708740 | tf_op jit(solution)/shard_map/reduce_sum | solution.py:56
  438.6 0.0 copy-done.6
  438.6 0.0 copy-done.10
  438.6 3.9 fusion.25
  442.4 4.0 convolution_convert_fusion
  446.4 64.1 %psum.23 = f32[]{:T(128)} all-reduce(f32[]{:T(128)} %get-tuple-element.13), channel_id=1, replica_groups=mesh['dp'=4,'mp'=32] {'dp','mp'}, use_global_device_ids=true, to_apply=%region_7.0 | all-reduce | flops 1 | bytes 8 | tf_op jit(solution)/shard_map/psum | solution.py:54
  510.5 0.6 neg.7
  512.4 6.1 %convolution_convert_fusion.1 = bf16[3584,512]{1,0:T(8,128)(2,1)} fusion(bf16[3584,512]{0,1:T(8,128)(2,1)} %all-gather.2.cloned.1.call-done, bf16[512,512]{1,0:T(8,128)(2,1)} %get-tuple-element.11), kind=kOutput, calls=%fused_computation.4 | convolution fusion | flops 1880883200 | bytes 7864320 | tf_op jit(solution)/shard_map/dot_general | solution.py:73
  (2 shorter events, 0.0 us)
Async XLA Ops:
  7.2 31.9 %copy-start = (bf16[448,3584]{1,0:T(8,128)(2,1)S(1)}, bf16[448,3584]{1,0:T(8,128)(2,1)}, u32[]{:S(2)}) copy-start(bf16[448,3584]{1,0:T(8,128)(2,1)} %param.16) | copy-start | bytes 9633796
  7.2 116.7 %reduce-scatter.4.cloned.1.call-start = ((), (), s32[]{:S(2)}) async-start(), calls=%async_computation.3 | async-start | bytes 1892352 | tf_op jit(solution)/shard_map/reduce_scatter | solution.py:32
  35.1 0.9 copy-start.1
  35.1 4.0 copy-start.3
  45.1 144.2 %copy-start.2 = (bf16[128,112]{0,1:T(8,128)(2,1)S(1)}, bf16[128,112]{0,1:T(8,128)(2,1)}, u32[]{:S(2)}) copy-start(bf16[128,112]{0,1:T(8,128)(2,1)} %param.11) | copy-start | bytes 86020
  47.8 213.1 %copy-start.7 = (f32[512]{0:T(512)S(1)}, f32[512]{0:T(512)}, u32[]{:S(2)}) copy-start(f32[512]{0:T(512)} %param.18) | copy-start | bytes 6148
  47.8 213.1 %all-gather.2.cloned.1.call-start = ((), (), s32[]{:S(2)}) async-start(), calls=%async_computation.1 | async-start | bytes 4587520 | tf_op jit(solution)/shard_map/all_gather | solution.py:46
  218.1 49.1 %copy-start.8 = (f32[512]{0:T(512)S(1)}, f32[512]{0:T(512)}, u32[]{:S(2)}) copy-start(f32[512]{0:T(512)} %param.19) | copy-start | bytes 6148
  218.1 214.5 %all-reduce.2.cloned.1.call-start = ((), (), s32[]{:S(2)}) async-start(), calls=%async_computation.2 | async-start | bytes 14680064 | tf_op jit(solution)/shard_map/psum | solution.py:54
  260.9 6.3 %copy-start.5 = (bf16[512,3584]{1,0:T(8,128)(2,1)S(1)}, bf16[512,3584]{1,0:T(8,128)(2,1)}, u32[]{:S(2)}) copy-start(bf16[512,3584]{1,0:T(8,128)(2,1)} %param.20) | copy-start | bytes 11010052
  266.3 1.0 copy-start.9
  272.4 160.2 %copy-start.4 = (f32[3584]{0:T(1024)S(1)}, f32[3584]{0:T(1024)}, u32[]{:S(2)}) copy-start(f32[3584]{0:T(1024)} %param.21) | copy-start | bytes 43012
  432.6 6.0 %copy-start.6 = (bf16[512,3584]{1,0:T(8,128)(2,1)S(1)}, bf16[512,3584]{1,0:T(8,128)(2,1)}, u32[]{:S(2)}) copy-start(bf16[512,3584]{1,0:T(8,128)(2,1)} %param.20) | copy-start | bytes 11010052
  432.6 6.0 %copy-start.10 = (f32[512,512]{1,0:T(8,128)S(1)}, f32[512,512]{1,0:T(8,128)}, u32[]{:S(2)}) copy-start(f32[512,512]{1,0:T(8,128)} %copy-done.9) | copy-start | bytes 3145732
Sparse Core Ops, SparseCore 0:
  47.9 75.9 reduce-scatter.3
  218.2 42.6 all-gather.1
  272.5 160.0 all-reduce.1
where the time goes:
time: 527 us; the launch traced here: 526 us
  waiting for transfers between devices  278 us (53%)
  blocking collectives  182 us (35%)
  matrix products  33.4 us (6%)
  between operations  16.3 us (3%)
  local copies, waits for them, and re-layouts  8.05 us (2%)
  other arithmetic  8.04 us (2%)
    psum x1, waiting for transfers between devices, local(): recon_all, gate_total = lax.psum((recon_part, gate_part), ('dp', 'mp'))  160 us
    reduce_scatter x1, waiting for transfers between devices, local(): lax.psum_scatter(lax.dot_general(w_down, hidden, (((0,), (1,)), ((), ()))...  75.3 us
    psum x1, blocking collectives, local(): total_sq = lax.psum(jnp.sum(out_share * out_share, axis=0), 'mp')  64.3 us
    psum x1, blocking collectives, local(): recon_all, gate_total = lax.psum((recon_part, gate_part), ('dp', 'mp'))  64.1 us
    all_gather x1, waiting for transfers between devices, local(): h_cols = lax.all_gather(column_rows, 'dp', axis=1, tiled=True)  42.6 us
    all_gather x1, blocking collectives, local(): full_rows = lax.all_gather(residual_in, 'mp', axis=1, tiled=True)  27.9 us
    all_gather x1, blocking collectives, local(): lax.all_gather(mixed.astype(jnp.bfloat16), 'mp', axis=0, tiled=True)  25.7 us
  transfers between devices with their start and end apart: 3, of which 3 were waited for; matrix products, arithmetic and copies ran while one was open for 0% of the time, Pallas kernels for 0%

commit v1 on v0

--- a/solution.py
+++ b/solution.py
@@ -51,7 +51,9 @@
     recon_part = lax.dot_general(
         w_dec, feat_bf, (((0,), (1,)), ((), ())), preferred_element_type=jnp.float32
     )
-    recon_all, gate_total = lax.psum((recon_part, gate_part), ("dp", "mp"))
+    recon_all, gate_total = jax.lax.psum(
+        jax.lax.psum((recon_part, gate_part), axis_name="mp"), axis_name="dp"
+    )
     error_t = recon_all + b_dec[:, None] - h_cols.astype(jnp.float32)
     grad_bdec = jnp.sum(error_t, axis=1)
     square_total = jnp.sum(error_t * error_t)

time: 527 us -> 645 us (1.22)
  waiting for transfers between devices: 278 us -> 382 us
  blocking collectives: 182 us -> 189 us
    psum x1 -> x2, waiting for transfers between devices: 160 us -> 264 us  [the longest x1 146 us: local(): jax.lax.psum(jax.lax.psum((recon_part, gate_part), axis_name='mp'), axis_...]
    psum x1 -> x2, blocking collectives: 64.1 us -> 70.6 us  [the longest x1 63.5 us: local(): jax.lax.psum((recon_part, gate_part), axis_name='mp')]
  transfers between devices with their start and end apart: 3 -> 4, of which waited for: 3 -> 4; matrix products, arithmetic and copies ran while one was open for 0% -> 0% of each run, Pallas kernels for 0% -> 0%
where the time goes in v1:
time: 645 us; the launch traced here: 639 us
  waiting for transfers between devices  382 us (59%)
  blocking collectives  189 us (29%)
  matrix products  35.8 us (6%)
  between operations  16.3 us (3%)
  local copies, waits for them, and re-layouts  8.04 us (1%)
  other arithmetic  8.04 us (1%)
    psum x1, waiting for transfers between devices, local(): jax.lax.psum(jax.lax.psum((recon_part, gate_part), axis_name='mp'), axis_...  146 us
    psum x1, waiting for transfers between devices, local(): jax.lax.psum((recon_part, gate_part), axis_name='mp')  118 us
    reduce_scatter x1, waiting for transfers between devices, local(): lax.psum_scatter(lax.dot_general(w_down, hidden, (((0,), (1,)), ((), ()))...  75.3 us
    psum x1, blocking collectives, local(): total_sq = lax.psum(jnp.sum(out_share * out_share, axis=0), 'mp')  64.3 us
    psum x1, blocking collectives, local(): jax.lax.psum((recon_part, gate_part), axis_name='mp')  63.5 us
    all_gather x1, waiting for transfers between devices, local(): h_cols = lax.all_gather(column_rows, 'dp', axis=1, tiled=True)  42.7 us
    all_gather x1, blocking collectives, local(): full_rows = lax.all_gather(residual_in, 'mp', axis=1, tiled=True)  27.9 us
    all_gather x1, blocking collectives, local(): lax.all_gather(mixed.astype(jnp.bfloat16), 'mp', axis=0, tiled=True)  25.7 us
  transfers between devices with their start and end apart: 4, of which 4 were waited for; matrix products, arithmetic and copies ran while one was open for 0% of the time, Pallas kernels for 0%

profile of v1, /device:TPU:1, one launch (start us, length us, event | category | flops | bytes accessed | tf_op | source)
XLA Modules:
  0.0 639.1 jit_solution(1904153193180739053)
XLA Ops:
  7.2 0.0 copy-start
  7.2 0.0 reduce-scatter.4.cloned.1.call-start
  7.2 27.9 %all_gather.9 = bf16[128,3584]{0,1:T(8,128)(2,1)S(1)} all-gather(bf16[128,112]{0,1:T(8,128)(2,1)} %param.11), channel_id=1, replica_groups=mesh['dp'=4,'mp'=32] {'mp'}, dimensions={1}, use_global_device_ids=true | all-gather | bytes 946176 | tf_op jit(solution)/shard_map/all_gather | solution.py:20
  35.1 0.0 copy-start.1
  35.1 0.0 copy-start.4
  35.1 0.5 fusion.2
  35.6 0.4 copy-done.1
  36.0 3.1 fusion.20
  39.1 0.0 copy-done
  39.1 0.0 copy-done.4
  39.1 6.0 convolution_bitcast_fusion.1
  45.1 0.0 copy-start.3
  45.1 2.7 copy.23
  47.8 0.0 copy-start.8
  47.8 0.0 reduce-scatter.4.cloned.1.call-update
  47.8 0.0 all-gather.2.cloned.1.call-start
  47.9 0.8 dynamic_slice.3
  48.6 75.3 %reduce-scatter.4.cloned.1.call-done = f32[112,128]{1,0:T(8,128)} async-done(((f32[3584,128]{1,0:T(8,128)}), f32[112,128]{1,0:T(8,128)}) %reduce-scatter.4.cloned.1.call-update) | async-done | bytes 57360 | tf_op jit(solution)/shard_map/reduce_scatter | solution.py:32
  123.9 0.9 copy.24
  124.8 0.1 multiply_reduce_fusion.1
  124.9 64.3 %psum.35 = f32[128]{0:T(128)S(1)} all-reduce(f32[128]{0:T(128)S(1)} %multiply_reduce_fusion.1), channel_id=1, replica_groups=mesh['dp'=4,'mp'=32] {'mp'}, use_global_device_ids=true, to_apply=%region_3.0 | all-reduce | flops 128 | bytes 1024 | tf_op jit(solution)/shard_map/psum | solution.py:40
  189.3 0.0 copy-done.3
  189.3 0.9 fusion.23
  190.2 25.7 %all_gather.10 = bf16[3584,128]{1,0:T(8,128)(2,1)} all-gather(bf16[112,128]{1,0:T(8,128)(2,1)S(1)} %fusion.23), channel_id=1, replica_groups=mesh['dp'=4,'mp'=32] {'mp'}, dimensions={0}, use_global_device_ids=true | all-gather | bytes 946176 | tf_op jit(solution)/shard_map/all_gather | solution.py:45
  215.9 2.2 copy.22
  218.1 0.0 all-gather.2.cloned.1.call-update
  218.1 0.0 copy-start.9
  218.1 0.0 all-reduce.3.cloned.1.call-start
  218.2 42.7 %all-gather.2.cloned.1.call-done = bf16[3584,512]{0,1:T(8,128)(2,1)} async-done(((bf16[3584,128]{0,1:T(8,128)(2,1)}), bf16[3584,512]{0,1:T(8,128)(2,1)}) %all-gather.2.cloned.1.call-update) | async-done | bytes 3670032 | tf_op jit(solution)/shard_map/all_gather | solution.py:46
  260.9 0.0 copy-done.8
  260.9 0.0 copy-start.6
  260.9 5.3 convolution_add_fusion
  266.3 0.0 copy-start.10
  266.3 0.9 copy-done.10
  267.2 0.0 copy-done.9
  267.2 0.0 copy-done.6
  267.2 5.1 convolution_bitcast_fusion
  272.4 0.0 all-reduce.3.cloned.1.call-update
  272.4 0.2 all-reduce.5.cloned.1.call-start
  272.6 118.3 %all-reduce.3.cloned.1.call-done = f32[3584,512]{0,1:T(8,128)} async-done(((f32[3584,512]{0,1:T(8,128)}), f32[3584,512]{0,1:T(8,128)}) %all-reduce.3.cloned.1.call-update) | async-done | bytes 7340048 | tf_op jit(solution)/shard_map/psum | solution.py:55
  390.9 0.0 copy-start.5
  390.9 0.0 all-reduce.5.cloned.1.call-update
  390.9 145.7 %all-reduce.5.cloned.1.call-done = f32[3584,512]{0,1:T(8,128)} async-done(((f32[3584,512]{0,1:T(8,128)}), f32[3584,512]{0,1:T(8,128)}) %all-reduce.5.cloned.1.call-update) | async-done | bytes 7340048 | tf_op jit(solution)/shard_map/psum | solution.py:54
  536.7 0.0 copy-done.5
  536.7 0.0 copy-start.7
  536.7 0.0 copy-start.11
  536.7 5.9 fusion
  542.6 0.0 copy-start.2
  542.6 0.0 copy-done.7
  542.6 0.0 copy-done.11
  542.6 3.9 fusion.25
  546.5 0.0 copy-done.2
  546.5 63.5 %psum.38 = f32[]{:T(128)} all-reduce(f32[]{:T(128)} %get-tuple-element.13), channel_id=1, replica_groups=mesh['dp'=4,'mp'=32] {'mp'}, use_global_device_ids=true, to_apply=%region_8.0 | all-reduce | flops 1 | bytes 8 | tf_op jit(solution)/shard_map/psum | solution.py:55
  610.0 6.3 convolution_convert_fusion
  616.3 7.2 %psum.39 = f32[]{:T(128)} all-reduce(f32[]{:T(128)} %psum.38), channel_id=1, replica_groups=mesh['dp'=4,'mp'=32] {'dp'}, use_global_device_ids=true, to_apply=%region_9.0 | all-reduce | flops 1 | bytes 8 | tf_op jit(solution)/shard_map/psum | solution.py:54
  623.5 0.6 neg.7
  625.3 6.1 convolution_convert_fusion.1
  (2 shorter events, 0.0 us)
Async XLA Ops:
  7.2 31.9 %copy-start = (bf16[448,3584]{1,0:T(8,128)(2,1)S(1)}, bf16[448,3584]{1,0:T(8,128)(2,1)}, u32[]{:S(2)}) copy-start(bf16[448,3584]{1,0:T(8,128)(2,1)} %param.16) | copy-start | bytes 9633796
  7.2 116.7 %reduce-scatter.4.cloned.1.call-start = ((), (), s32[]{:S(2)}) async-start(), calls=%async_computation.4 | async-start | bytes 1892352 | tf_op jit(solution)/shard_map/reduce_scatter | solution.py:32
  35.1 0.9 copy-start.1
  35.1 4.0 copy-start.4
  45.1 144.2 %copy-start.3 = (bf16[128,112]{0,1:T(8,128)(2,1)S(1)}, bf16[128,112]{0,1:T(8,128)(2,1)}, u32[]{:S(2)}) copy-start(bf16[128,112]{0,1:T(8,128)(2,1)} %param.11) | copy-start | bytes 86020
  47.8 213.1 %copy-start.8 = (f32[512]{0:T(512)S(1)}, f32[512]{0:T(512)}, u32[]{:S(2)}) copy-start(f32[512]{0:T(512)} %param.18) | copy-start | bytes 6148
  47.8 213.1 %all-gather.2.cloned.1.call-start = ((), (), s32[]{:S(2)}) async-start(), calls=%async_computation.1 | async-start | bytes 4587520 | tf_op jit(solution)/shard_map/all_gather | solution.py:46
  218.1 49.1 %copy-start.9 = (f32[512]{0:T(512)S(1)}, f32[512]{0:T(512)}, u32[]{:S(2)}) copy-start(f32[512]{0:T(512)} %param.19) | copy-start | bytes 6148
  218.1 172.8 %all-reduce.3.cloned.1.call-start = ((), (), s32[]{:S(2)}) async-start(), calls=%async_computation.2 | async-start | bytes 14680064 | tf_op jit(solution)/shard_map/psum | solution.py:55
  260.9 6.3 copy-start.6
  266.3 1.0 copy-start.10
  272.4 264.3 %all-reduce.5.cloned.1.call-start = ((), (), s32[]{:S(2)}) async-start(), calls=%async_computation.3 | async-start | bytes 14680064 | tf_op jit(solution)/shard_map/psum | solution.py:54
  390.9 145.7 %copy-start.5 = (f32[3584]{0:T(1024)S(1)}, f32[3584]{0:T(1024)}, u32[]{:S(2)}) copy-start(f32[3584]{0:T(1024)} %param.21) | copy-start | bytes 43012
  536.7 6.0 copy-start.7
  536.7 6.0 copy-start.11
  542.6 3.9 copy-start.2
Sparse Core Ops, SparseCore 0:
  47.9 75.9 reduce-scatter.3
  218.2 42.6 all-gather.1
  272.5 118.3 all-reduce.2
  393.1 143.4 all-reduce.4
